TPU v7x, 32 devices: a whole 2x2x4 slice. The times are simulated.
32 devices in a mesh: section: 4 (over x, core), expert: 4 (over z), dp: 2 (over y).
Axes of the slice: x: 2, y: 2, z: 4, core: 2. Of those that a mesh axis runs over, the one named last changes fastest.
Arguments:
- fwd_sent: bfloat16 [4, 128, 3584], P('section', ('expert', 'dp')), may hold values from -6 to 6
- fwd_routes: int32 [4, 128, 1], P('section', ('expert', 'dp')), may hold values from 0 to 1; in each aligned block of 16 rows (0 to 15, 16 to 31, ..., all dimensions but the last counted through in order) at most 16 rows name the same one
- fwd_probs: float32 [4, 128, 1], P('section', ('expert', 'dp')), may hold values from 0.2 to 1.25
- backward_cotangent: bfloat16 [4, 128, 3584], P('section', ('expert', 'dp')), may hold values from -6 to 6
- bwd_routes: int32 [4, 128, 1], P('section', ('expert', 'dp')), may hold values from 0 to 1; in each aligned block of 16 rows (0 to 15, 16 to 31, ..., all dimensions but the last counted through in order) at most 16 rows name the same one
- bwd_probs: float32 [4, 128, 1], P('section', ('expert', 'dp')), may hold values from 0.2 to 1.25
- saved_pre: bfloat16 [4, 2, 64, 2, 2048], P('section', 'dp', None, None, 'expert'), may hold values from -6 to 6
- w_gate: bfloat16 [4, 3584, 2048], P('section', None, 'expert'), may hold values from -0.09375 to 0.09375
- w_up: bfloat16 [4, 3584, 2048], P('section', None, 'expert'), may hold values from -0.09375 to 0.09375
- w_down: bfloat16 [4, 2048, 3584], P('section', 'expert'), may hold values from -0.1875 to 0.1875
Outputs:
- fwd_next: bfloat16 [4, 128, 3584], P('section', ('expert', 'dp'))
- bwd_next: bfloat16 [4, 128, 3584], P('section', ('expert', 'dp'))
- expert_load: int32 [4, 4], P('section', 'expert')
Inputs may be any that keep to these rules, and one draw needn't show every extreme that they name: `fwd_routes`: among the rows of one device, no expert is named by more than 16 routes, a bound that some block reaches; a row names 1 different experts. `bwd_routes`: among the rows of one device, no expert is named by more than 16 routes, a bound that some block reaches; a row names 1 different experts.
All inputs are finite; a program needn't handle non-finite values.
Results may differ from a plain program's by a relative error of at most 0.007.
Values may be sent and summed in bfloat16 or wider, within the bound.
A program may use at most 64 MiB of HBM per device.

v0:
```python
import jax
import jax.numpy as jnp
from jax import lax
from jax.sharding import PartitionSpec as P


def from_behind(array, axis, by):
    length = lax.axis_size(axis)
    return lax.ppermute(array, axis, [(i, (i + by) % length) for i in range(length)])


def slot_tables(routes, probs, exp_count, capacity):
    slot_count = exp_count * capacity
    flat_routes = routes.reshape(-1)
    onehot = (flat_routes[:, None] == jnp.arange(exp_count, dtype=jnp.int32)[None, :]).astype(
        jnp.int32
    )
    before = jnp.cumsum(onehot, axis=0) - onehot
    position = jnp.sum(before * onehot, axis=1)
    slot_ids = flat_routes * capacity + position
    matches = (slot_ids[:, None] == jnp.arange(slot_count, dtype=jnp.int32)[None, :]).astype(
        jnp.float32
    )
    matches = matches.reshape(routes.shape[0], routes.shape[1], slot_count)
    placing = jnp.sum(matches, axis=1)
    weighing = jnp.sum(matches * probs[:, :, None], axis=1)
    counted = jnp.sum(onehot, axis=0)
    return (placing, weighing, counted)


def shards(
    fwd_sent,
    fwd_routes,
    fwd_probs,
    backward_cotangent,
    bwd_routes,
    bwd_probs,
    saved_pre,
    w_gate,
    w_up,
    w_down,
):
    experts = lax.axis_size("expert")
    sharing = min(4, experts // 2)
    exp_count = experts // sharing
    token_rows = fwd_sent.shape[1]
    top_count = fwd_routes.shape[2]
    capacity = min(token_rows, max(2, 2 * token_rows * top_count // exp_count))
    slot_count = experts * capacity
    arrived = from_behind(fwd_sent, "section", 1)[0]
    gate_mat = w_gate[0]
    up_mat = w_up[0]
    down_mat = w_down[0]
    stored = saved_pre[0, 0]
    cotangent = backward_cotangent[0]
    fwd_place, fwd_weigh, fwd_count = slot_tables(fwd_routes[0], fwd_probs[0], exp_count, capacity)
    bwd_place, bwd_weigh, bwd_count = slot_tables(bwd_routes[0], bwd_probs[0], exp_count, capacity)

    def forward_rows(slot_rows):
        gate_pre = jnp.dot(slot_rows, gate_mat, preferred_element_type=jnp.float32)
        up_pre = jnp.dot(slot_rows, up_mat, preferred_element_type=jnp.float32)
        hidden_state = (jax.nn.silu(gate_pre) * up_pre).astype(jnp.bfloat16)
        return jnp.dot(hidden_state, down_mat, preferred_element_type=jnp.float32).astype(
            jnp.bfloat16
        )

    def backward_rows(slot_rows):
        contract = (((1,), (1,)), ((), ()))
        grad_hidden = lax.dot_general(
            slot_rows, down_mat, contract, preferred_element_type=jnp.float32
        )
        saved_gate = stored[:, 0].astype(jnp.float32)
        saved_up = stored[:, 1].astype(jnp.float32)
        sigma = jax.nn.sigmoid(saved_gate)
        grad_gate = (grad_hidden * saved_up * sigma * (1.0 + saved_gate * (1.0 - sigma))).astype(
            jnp.bfloat16
        )
        grad_up = (grad_hidden * saved_gate * sigma).astype(jnp.bfloat16)
        summed = lax.dot_general(grad_gate, gate_mat, contract, preferred_element_type=jnp.float32)
        summed = summed + lax.dot_general(
            grad_up, up_mat, contract, preferred_element_type=jnp.float32
        )
        return summed.astype(jnp.bfloat16)

    def send_rows(tokens, placing):
        width = tokens.shape[1]
        outgoing = jnp.dot(
            placing.T.astype(jnp.bfloat16), tokens, preferred_element_type=jnp.float32
        )
        outgoing = outgoing.astype(jnp.bfloat16).reshape(exp_count, 1, capacity, width)
        outgoing = jnp.broadcast_to(outgoing, (exp_count, sharing, capacity, width)).reshape(
            experts, capacity, width
        )
        received = lax.all_to_all(outgoing, "expert", split_axis=0, concat_axis=0, tiled=True)
        owned = jnp.zeros((), jnp.int32)
        return (received.reshape(slot_count, width), owned)

    def finish_rows(received, compute):
        width = received.shape[1]
        result_list = compute(received)
        returned = lax.all_to_all(
            result_list.reshape(experts, capacity, width),
            "expert",
            split_axis=0,
            concat_axis=0,
            tiled=True,
        )
        gathered = jnp.sum(
            returned.reshape(exp_count, sharing, capacity, width).astype(jnp.float32), axis=1
        )
        return gathered.reshape(exp_count * capacity, width)

    fwd_rows, fwd_owned = send_rows(arrived, fwd_place)
    fwd_back = finish_rows(fwd_rows, forward_rows)
    bwd_rows, bwd_owned = send_rows(cotangent, bwd_place)
    bwd_back = finish_rows(bwd_rows, backward_rows)
    fwd_next = arrived.astype(jnp.float32) + jnp.dot(
        fwd_weigh, fwd_back, precision=lax.Precision.HIGHEST
    )
    bwd_next = cotangent.astype(jnp.float32) + jnp.dot(
        bwd_weigh, bwd_back, precision=lax.Precision.HIGHEST
    )
    totals = lax.psum(fwd_count + bwd_count, ("expert", "dp"))
    expert_load = lax.dynamic_slice_in_dim(totals, lax.axis_index("expert") // sharing, 1)[0]
    return (
        fwd_next.astype(jnp.bfloat16)[None],
        bwd_next.astype(jnp.bfloat16)[None],
        expert_load.reshape(1, 1),
    )


def solution(mesh):
    in_specs = (
        P("section", ("expert", "dp"), None),
        P("section", ("expert", "dp"), None),
        P("section", ("expert", "dp"), None),
        P("section", ("expert", "dp"), None),
        P("section", ("expert", "dp"), None),
        P("section", ("expert", "dp"), None),
        P("section", "dp", None, None, "expert"),
        P("section", None, "expert"),
        P("section", None, "expert"),
        P("section", "expert", None),
    )
    out_specs = (
        P("section", ("expert", "dp"), None),
        P("section", ("expert", "dp"), None),
        P("section", "expert"),
    )
    return jax.shard_map(shards, mesh=mesh, in_specs=in_specs, out_specs=out_specs, check_vma=False)
```

profile of v0, /device:TPU:0, one launch (start us, length us, event | category | flops | bytes accessed | tf_op | source)
XLA Modules:
  0.0 76.4 jit_solution(12552506827635663010)
XLA Ops:
  0.6 0.7 fusion.46
  1.4 0.7 fusion.44
  2.2 0.9 %fusion.47 = (s32[2]{0:T(128)S(1)}, s32[16]{0:T(128)S(1)}, s32[16]{0:T(128)S(1)}, s32[2]{0:T(128)S(1)}) fusion(s32[16]{0:T(128)} %bitcast.97, s32[16,2]{1,0:T(8,128)S(1)} %reduce_window_sum.17, s32[16,2]{1,0:T(8,128)S(1)} %reduce_window_sum.18, s32[16]{0:T(128)} %bitcast.95), kind=kLoop, calls=%fused_computation.64 | loop fusion | flops 348 | bytes 528 | tf_op jit(solution)/shard_map/reduce_sum | solution.py:27
  3.0 0.7 multiply_add_fusion
  3.7 1.1 %convolution_convert_fusion.1 = bf16[32,3584]{1,0:T(8,128)(2,1)S(1)} fusion(bf16[1,16,3584]{2,1,0:T(8,128)(2,1)} %param.13, s32[16]{0:T(128)S(1)} %multiply_add_fusion), kind=kOutput, calls=%fused_computation.3 | convolution fusion | flops 3786240 | bytes 344128 | tf_op jit(solution)/shard_map/dot_general | solution.py:87
  4.8 0.8 %broadcast_in_dim.30 = bf16[2,2,16,3584]{3,2,1,0:T(8,128)(2,1)} broadcast(bf16[2,16,3584]{2,1,0:T(8,128)(2,1)S(1)} %bitcast.89), dimensions={0,2,3} | broadcast | bytes 688128 | tf_op jit(solution)/shard_map/broadcast_in_dim | solution.py:91
  5.6 6.3 %all-to-all-start.2 = ((bf16[4,16,3584]{2,1,0:T(8,128)(2,1)}), bf16[4,16,3584]{2,1,0:T(8,128)(2,1)S(1)}, u32[]{:S(2)}, u32[]{:S(2)}) async-start(bf16[4,16,3584]{2,1,0:T(8,128)(2,1)} %bitcast.19), calls=%async_computation.2 | async-start | bytes 917504 | tf_op jit(solution)/shard_map/all_to_all | solution.py:94
  11.9 13.9 %psum.7 = s32[2]{0:T(128)S(1)} all-reduce(s32[2]{0:T(128)S(1)} %add.50), channel_id=1, replica_groups=mesh['section'=4,'expert'=4,'dp'=2] {'expert','dp'}, use_global_device_ids=true, to_apply=%region_8.9 | all-reduce | flops 2 | bytes 16 | tf_op jit(solution)/shard_map/psum | solution.py:123
  25.8 0.9 %copy.15 = bf16[1,1,64,2,512]{4,2,3,1,0:T(8,128)(2,1)S(1)} copy(bf16[1,1,64,2,512]{4,3,2,1,0:T(2,128)(2,1)} %param.16) | data formatting | bytes 262144 | tf_op args[6]
  27.3 0.7 multiply_add_fusion.1
  28.1 0.8 %broadcast_in_dim.13 = bf16[2,2,16,3584]{3,2,1,0:T(8,128)(2,1)} broadcast(bf16[2,16,3584]{2,1,0:T(8,128)(2,1)S(1)} %bitcast.88), dimensions={0,2,3} | broadcast | bytes 688128 | tf_op jit(solution)/shard_map/broadcast_in_dim | solution.py:91
  28.9 3.5 %all-to-all-start = ((bf16[4,16,3584]{2,1,0:T(8,128)(2,1)}), bf16[4,16,3584]{2,1,0:T(8,128)(2,1)S(1)}, u32[]{:S(2)}, u32[]{:S(2)}) async-start(bf16[4,16,3584]{2,1,0:T(8,128)(2,1)} %bitcast.5), calls=%async_computation | async-start | bytes 917504 | tf_op jit(solution)/shard_map/all_to_all | solution.py:94
  32.4 3.4 %fusion.3 = f32[64,512]{1,0:T(8,128)S(1)} fusion(bf16[64,3584]{1,0:T(8,128)(2,1)S(1)} %bitcast.85, bf16[1,512,3584]{2,1,0:T(8,128)(2,1)} %param.19), kind=kOutput, calls=%fused_computation.8 | convolution fusion | flops 234881024 | bytes 4259840 | tf_op jit(solution)/shard_map/dot_general | solution.py:69
  35.9 1.2 %fusion.9 = f32[64,3584]{1,0:T(8,128)S(1)} fusion(bf16[1,3584,512]{2,1,0:T(8,128)(2,1)S(1)} %copy-done.1, f32[64,512]{1,0:T(8,128)S(1)} %fusion.3, bf16[64,2,512]{2,0,1:T(8,128)(2,1)S(1)} %bitcast.90), kind=kOutput, calls=%fused_computation.14 | convolution fusion | flops 235274240 | bytes 4849664 | tf_op jit(solution)/shard_map/dot_general | solution.py:79
  37.1 2.0 %fusion = bf16[64,3584]{1,0:T(8,128)(2,1)} fusion(f32[64,3584]{1,0:T(8,128)S(1)} %fusion.9, bf16[1,3584,512]{2,1,0:T(8,128)(2,1)S(1)} %copy-done, f32[64,512]{1,0:T(8,128)S(1)} %fusion.3, bf16[64,2,512]{2,0,1:T(8,128)(2,1)S(1)} %bitcast.91), kind=kOutput, calls=%fused_computation.2 | convolution fusion | flops 235569152 | bytes 5242880 | tf_op jit(solution)/shard_map/dot_general | solution.py:80
  39.1 5.3 %all-to-all-done = bf16[4,16,3584]{2,1,0:T(8,128)(2,1)S(1)} async-done(((bf16[4,16,3584]{2,1,0:T(8,128)(2,1)}), bf16[4,16,3584]{2,1,0:T(8,128)(2,1)S(1)}, u32[]{:S(2)}, u32[]{:S(2)}) %all-to-all-start) | async-done | bytes 458784 | tf_op jit(solution)/shard_map/all_to_all | solution.py:94
  44.4 3.5 %all-to-all-start.3 = ((bf16[4,16,3584]{2,1,0:T(8,128)(2,1)}), bf16[4,16,3584]{2,1,0:T(8,128)(2,1)S(1)}, u32[]{:S(2)}, u32[]{:S(2)}) async-start(bf16[4,16,3584]{2,1,0:T(8,128)(2,1)} %bitcast.25), calls=%async_computation.3 | async-start | bytes 917504 | tf_op jit(solution)/shard_map/all_to_all | solution.py:101
  47.9 2.8 %fusion.11 = f32[64,512]{1,0:T(8,128)S(1)} fusion(bf16[64,3584]{1,0:T(8,128)(2,1)S(1)} %bitcast.83, bf16[1,3584,512]{2,1,0:T(8,128)(2,1)} %param.17), kind=kOutput, calls=%fused_computation.16 | convolution fusion | flops 234881024 | bytes 4259840 | tf_op jit(solution)/shard_map/dot_general | solution.py:60
  50.7 5.4 %convolution_convert_fusion = bf16[64,3584]{1,0:T(8,128)(2,1)} fusion(bf16[1,512,3584]{2,1,0:T(8,128)(2,1)} %param.19, bf16[64,3584]{1,0:T(8,128)(2,1)S(1)} %bitcast.84, bf16[1,3584,512]{2,1,0:T(8,128)(2,1)} %param.18, f32[64,512]{1,0:T(8,128)S(1)} %fusion.11), kind=kOutput, calls=%fused_computation.1 | convolution fusion | flops 470188032 | bytes 8388608 | tf_op jit(solution)/shard_map/dot_general | solution.py:63
  56.1 3.7 %all-to-all-done.3 = bf16[4,16,3584]{2,1,0:T(8,128)(2,1)S(1)} async-done(((bf16[4,16,3584]{2,1,0:T(8,128)(2,1)}), bf16[4,16,3584]{2,1,0:T(8,128)(2,1)S(1)}, u32[]{:S(2)}, u32[]{:S(2)}) %all-to-all-start.3) | async-done | bytes 458784 | tf_op jit(solution)/shard_map/all_to_all | solution.py:101
  59.8 3.5 %all-to-all-start.1 = ((bf16[4,16,3584]{2,1,0:T(8,128)(2,1)}), bf16[4,16,3584]{2,1,0:T(8,128)(2,1)S(1)}, u32[]{:S(2)}, u32[]{:S(2)}) async-start(bf16[4,16,3584]{2,1,0:T(8,128)(2,1)} %bitcast.10), calls=%async_computation.1 | async-start | bytes 917504 | tf_op jit(solution)/shard_map/all_to_all | solution.py:101
  63.6 1.0 %fusion.2 = bf16[1,16,3584]{2,1,0:T(8,128)(2,1)} fusion(f32[16,32]{1,0:T(8,128)S(1)} %bitcast.93, f32[32,3584]{1,0:T(8,128)S(1)} %bitcast.87, bf16[1,16,3584]{2,1,0:T(8,128)(2,1)S(1)} %copy-done.2), kind=kOutput, calls=%fused_computation.7 | convolution fusion | flops 22192128 | bytes 690176 | tf_op jit(solution)/shard_map/dot_general | solution.py:120
  64.6 10.7 %all-to-all-done.1 = bf16[4,16,3584]{2,1,0:T(8,128)(2,1)S(1)} async-done(((bf16[4,16,3584]{2,1,0:T(8,128)(2,1)}), bf16[4,16,3584]{2,1,0:T(8,128)(2,1)S(1)}, u32[]{:S(2)}, u32[]{:S(2)}) %all-to-all-start.1) | async-done | bytes 458784 | tf_op jit(solution)/shard_map/all_to_all | solution.py:101
  75.4 1.0 %fusion.35 = bf16[1,16,3584]{2,1,0:T(8,128)(2,1)} fusion(bf16[1,16,3584]{2,1,0:T(8,128)(2,1)S(1)} %collective-permute-done, f32[16,32]{1,0:T(8,128)S(1)} %bitcast.92, f32[32,3584]{1,0:T(8,128)S(1)} %bitcast.86), kind=kOutput, calls=%fused_computation.42 | convolution fusion | flops 22192128 | bytes 690176 | tf_op jit(solution)/shard_map/dot_general | solution.py:117
  (22 shorter events, 1.2 us)
Async XLA Ops:
  5.6 22.6 %all-to-all-start.2 = ((bf16[4,16,3584]{2,1,0:T(8,128)(2,1)}), bf16[4,16,3584]{2,1,0:T(8,128)(2,1)S(1)}, u32[]{:S(2)}, u32[]{:S(2)}) async-start(bf16[4,16,3584]{2,1,0:T(8,128)(2,1)} %bitcast.19), calls=%async_computation.2 | async-start | bytes 917504 | tf_op jit(solution)/shard_map/all_to_all | solution.py:94
  11.9 16.0 %collective-permute-start = (bf16[1,16,3584]{2,1,0:T(8,128)(2,1)}, bf16[1,16,3584]{2,1,0:T(8,128)(2,1)S(1)}, u32[]{:S(2)}, u32[]{:S(2)}) collective-permute-start(bf16[1,16,3584]{2,1,0:T(8,128)(2,1)} %param.10), channel_id=1, source_target_pairs={{0,8},{8,16},{16,24},{24,0},{1,9},{9,17},{17,25},{25,1},{2,10},{10... | collective-permute-start | bytes 344072 | tf_op jit(solution)/shard_map/ppermute | solution.py:9
  28.9 15.4 %all-to-all-start = ((bf16[4,16,3584]{2,1,0:T(8,128)(2,1)}), bf16[4,16,3584]{2,1,0:T(8,128)(2,1)S(1)}, u32[]{:S(2)}, u32[]{:S(2)}) async-start(bf16[4,16,3584]{2,1,0:T(8,128)(2,1)} %bitcast.5), calls=%async_computation | async-start | bytes 917504 | tf_op jit(solution)/shard_map/all_to_all | solution.py:94
  32.4 3.4 %copy-start.1 = (bf16[1,3584,512]{2,1,0:T(8,128)(2,1)S(1)}, bf16[1,3584,512]{2,1,0:T(8,128)(2,1)}, u32[]{:S(2)}) copy-start(bf16[1,3584,512]{2,1,0:T(8,128)(2,1)} %param.17) | copy-start | bytes 11010052
  32.4 4.6 %copy-start = (bf16[1,3584,512]{2,1,0:T(8,128)(2,1)S(1)}, bf16[1,3584,512]{2,1,0:T(8,128)(2,1)}, u32[]{:S(2)}) copy-start(bf16[1,3584,512]{2,1,0:T(8,128)(2,1)} %param.18) | copy-start | bytes 11010052
  44.4 15.4 %all-to-all-start.3 = ((bf16[4,16,3584]{2,1,0:T(8,128)(2,1)}), bf16[4,16,3584]{2,1,0:T(8,128)(2,1)S(1)}, u32[]{:S(2)}, u32[]{:S(2)}) async-start(bf16[4,16,3584]{2,1,0:T(8,128)(2,1)} %bitcast.25), calls=%async_computation.3 | async-start | bytes 917504 | tf_op jit(solution)/shard_map/all_to_all | solution.py:101
  50.6 12.7 %copy-start.3 = (f32[1,16,1]{1,2,0:T(1,128)S(1)}, f32[1,16,1]{1,2,0:T(1,128)}, u32[]{:S(2)}) copy-start(f32[1,16,1]{1,2,0:T(1,128)} %param.12) | copy-start | bytes 196
  50.7 12.8 %copy-start.4 = (f32[1,16,1]{1,2,0:T(1,128)S(1)}, f32[1,16,1]{1,2,0:T(1,128)}, u32[]{:S(2)}) copy-start(f32[1,16,1]{1,2,0:T(1,128)} %param.15) | copy-start | bytes 196
  50.7 12.9 %copy-start.2 = (bf16[1,16,3584]{2,1,0:T(8,128)(2,1)S(1)}, bf16[1,16,3584]{2,1,0:T(8,128)(2,1)}, u32[]{:S(2)}) copy-start(bf16[1,16,3584]{2,1,0:T(8,128)(2,1)} %param.13) | copy-start | bytes 344068
  59.8 15.5 %all-to-all-start.1 = ((bf16[4,16,3584]{2,1,0:T(8,128)(2,1)}), bf16[4,16,3584]{2,1,0:T(8,128)(2,1)S(1)}, u32[]{:S(2)}, u32[]{:S(2)}) async-start(bf16[4,16,3584]{2,1,0:T(8,128)(2,1)} %bitcast.10), calls=%async_computation.1 | async-start | bytes 917504 | tf_op jit(solution)/shard_map/all_to_all | solution.py:101
where the time goes:
time: 76.9 us; the launch traced here: 76.4 us
  waiting for transfers between devices  19.7 us (26%)
  matrix products  18.1 us (24%)
  starting transfers between devices  16.7 us (22%)
  blocking collectives  13.9 us (18%)
  other arithmetic  4.03 us (5%)
  local copies, waits for them, and re-layouts  3.15 us (4%)
  between operations  0.82 us (1%)
    all_to_all x2, waiting for transfers between devices, finish_rows(): lax.all_to_all(result_list.reshape(experts, capacity, width), 'expert', s...  14.4 us
    psum x1, blocking collectives, shards(): totals = lax.psum(fwd_count + bwd_count, ('expert', 'dp'))  13.9 us
    all_to_all x2, starting transfers between devices, send_rows(): lax.all_to_all(outgoing, 'expert', split_axis=0, concat_axis=0, tiled=True)  9.79 us
    all_to_all x2, starting transfers between devices, finish_rows(): lax.all_to_all(result_list.reshape(experts, capacity, width), 'expert', s...  6.93 us
    dot_general x1, matrix products, forward_rows(): jnp.dot(hidden_state, down_mat, preferred_element_type=jnp.float32)  5.43 us
    all_to_all x2, waiting for transfers between devices, send_rows(): lax.all_to_all(outgoing, 'expert', split_axis=0, concat_axis=0, tiled=True)  5.31 us
    dot_general x1, matrix products, backward_rows(): lax.dot_general(slot_rows, down_mat, contract, preferred_element_type=jnp...  3.4 us
    dot_general x1, matrix products, forward_rows(): gate_pre = jnp.dot(slot_rows, gate_mat, preferred_element_type=jnp.float32)  2.78 us
  transfers between devices with their start and end apart: 5, of which 3 were waited for; matrix products, arithmetic and copies ran while one was open for 24% of the time, Pallas kernels for 0%

commit v1 on v0

--- a/solution.py
+++ b/solution.py
@@ -1,7 +1,17 @@
+import functools
+
 import jax
 import jax.numpy as jnp
 from jax import lax
+from jax.experimental import pallas as pl
+from jax.experimental.pallas import tpu as pltpu
 from jax.sharding import PartitionSpec as P
+
+MESH = pl.DeviceIdType.MESH
+LEFT, RIGHT = 0, 1
+FWD, BWD = 0, 1
+GATHER_CHUNKS = 2
+RETURN_CHUNKS = 2
 
 
 def from_behind(array, axis, by):
@@ -26,6 +36,474 @@
     weighing = jnp.sum(matches * probs[:, :, None], axis=1)
     counted = jnp.sum(onehot, axis=0)
     return (placing, weighing, counted)
+
+
+def cuts(width, wanted):
+    count = max(c for c in range(1, wanted + 1) if width % (c * 128) == 0)
+    step = width // count
+    return [pl.ds(i * step, step) for i in range(count)]
+
+
+def relay_kernel(
+    size,
+    x_ref,
+    cot_ref,
+    f_routes,
+    b_routes,
+    f_probs,
+    b_probs,
+    saved_hbm,
+    gate_hbm,
+    up_hbm,
+    down_hbm,
+    f_out,
+    b_out,
+    load_out,
+    gate_w,
+    up_w,
+    down_w,
+    saved,
+    rows_all,
+    meta,
+    from_right,
+    from_left,
+    going,
+    part,
+    hidden_acc,
+    mid,
+    w_sem,
+    shift_send,
+    shift_recv,
+    meta_send,
+    meta_recv,
+    g_send,
+    g_recv,
+    r_send,
+    r_recv,
+):
+    n, n_dp, n_sec, sharing, cap, rows = size
+    group = n * n_dp
+    width = cot_ref.shape[1]
+    me = lax.axis_index("expert")
+    dp = lax.axis_index("dp")
+    sec = lax.axis_index("section")
+    lin = me * n_dp + dp
+    g_cuts = cuts(width, GATHER_CHUNKS)
+    r_cuts = cuts(width, RETURN_CHUNKS)
+    contract_last = (((1,), (1,)), ((), ()))
+
+    loads = [
+        pltpu.make_async_copy(down_hbm, down_w, w_sem.at[0]),
+        pltpu.make_async_copy(saved_hbm, saved, w_sem.at[1]),
+        pltpu.make_async_copy(gate_hbm, gate_w, w_sem.at[2]),
+        pltpu.make_async_copy(up_hbm, up_w, w_sem.at[3]),
+    ]
+    for load in loads:
+        load.start()
+
+    def place(block):
+        return pl.ds(pl.multiple_of(block * rows, rows), rows)
+
+    barrier = pltpu.get_barrier_semaphore()
+
+    def peer(off):
+        other = lax.rem(lin + off, group)
+        return {"expert": lax.div(other, n_dp), "dp": lax.rem(other, n_dp)}
+
+    for off in range(1, group):
+        pl.semaphore_signal(barrier, inc=1, device_id=peer(off), device_id_type=MESH)
+    pl.semaphore_signal(
+        barrier,
+        inc=1,
+        device_id={"section": lax.rem(sec + n_sec - 1, n_sec)},
+        device_id_type=MESH,
+    )
+
+    at_row = lax.broadcasted_iota(jnp.int32, (rows, rows), 0)
+    at_col = lax.broadcasted_iota(jnp.int32, (rows, rows), 1)
+    eye = at_row == at_col
+    meta[lin] = jnp.zeros(meta.shape[1:], jnp.float32)
+    for span, routes in ((FWD, f_routes), (BWD, b_routes)):
+        named = jnp.broadcast_to(routes[...].astype(jnp.float32), (rows, rows))
+        named_row = jnp.sum(jnp.where(eye, named, 0.0), axis=0, keepdims=True)
+        earlier = jnp.where((named == named_row) & (at_row < at_col), 1.0, 0.0)
+        slot = named_row * cap + jnp.sum(earlier, axis=0, keepdims=True)
+        meta[lin, span : span + 1, 0:rows] = slot
+    rows_all[BWD, place(me), :] = cot_ref[...]
+
+    pl.semaphore_wait(barrier, group)
+
+    def gather_copy(span, way, hop, chunk):
+        block = me - (hop - 1) if way == RIGHT else me + (hop - 1)
+        there = me + 1 if way == RIGHT else me - 1
+        piece = rows_all.at[span, place(block), g_cuts[chunk]]
+        return pltpu.make_async_remote_copy(
+            src_ref=piece,
+            dst_ref=piece,
+            send_sem=g_send.at[span, way, hop - 1, chunk],
+            recv_sem=g_recv.at[span, way, hop - 1, chunk],
+            device_id={"expert": there},
+            device_id_type=MESH,
+        )
+
+    def gather_sends(way, hop):
+        if way == RIGHT:
+            return (me >= hop - 1) & (me < n - 1)
+        return (me <= n - hop) & (me > 0)
+
+    def gather_wait(span, way, hop, chunk):
+        block = me - hop if way == RIGHT else me + hop
+        there = me - 1 if way == RIGHT else me + 1
+        piece = rows_all.at[span, place(block), g_cuts[chunk]]
+        pltpu.make_async_remote_copy(
+            src_ref=piece,
+            dst_ref=piece,
+            send_sem=g_send.at[span, way, hop - 1, chunk],
+            recv_sem=g_recv.at[span, way, hop - 1, chunk],
+            device_id={"expert": there},
+            device_id_type=MESH,
+        ).wait_recv()
+
+    def gather_start(span, hop):
+        for chunk in range(len(g_cuts)):
+            for way in (LEFT, RIGHT):
+
+                @pl.when(gather_sends(way, hop))
+                def _():
+                    gather_copy(span, way, hop, chunk).start()
+
+    def gather_step(span, hop, chunk):
+        for way in (LEFT, RIGHT):
+            there = me >= hop if way == RIGHT else me + hop < n
+
+            @pl.when(there)
+            def _():
+                gather_wait(span, way, hop, chunk)
+
+            if hop < n - 1:
+
+                @pl.when(gather_sends(way, hop + 1))
+                def _():
+                    gather_copy(span, way, hop + 1, chunk).start()
+
+    def return_copy(span, way, block, chunk):
+        landing = from_left if way == RIGHT else from_right
+        there = me + 1 if way == RIGHT else me - 1
+        spot = pl.ds(block * rows, rows)
+        return pltpu.make_async_remote_copy(
+            src_ref=going.at[span, spot, r_cuts[chunk]],
+            dst_ref=landing.at[span, spot, r_cuts[chunk]],
+            send_sem=r_send.at[span, way, block, chunk],
+            recv_sem=r_recv.at[span, way, block, chunk],
+            device_id={"expert": there},
+            device_id_type=MESH,
+        )
+
+    def return_wait(span, way, block, chunk):
+        landing = from_left if way == RIGHT else from_right
+        there = me - 1 if way == RIGHT else me + 1
+        piece = landing.at[span, place(block), r_cuts[chunk]]
+        pltpu.make_async_remote_copy(
+            src_ref=piece,
+            dst_ref=piece,
+            send_sem=r_send.at[span, way, block, chunk],
+            recv_sem=r_recv.at[span, way, block, chunk],
+            device_id={"expert": there},
+            device_id_type=MESH,
+        ).wait_recv()
+
+    def return_step(span, hop, chunk):
+        for way in (LEFT, RIGHT):
+            at = n - 1 - hop if way == LEFT else hop
+            blocks = range(at) if way == LEFT else range(n - 1, at, -1)
+            landing = from_left if way == RIGHT else from_right
+
+            @pl.when(me == at)
+            def _():
+                for block in blocks:
+                    spot = pl.ds(block * rows, rows)
+                    total = part[span, spot, r_cuts[chunk]]
+                    if hop > 0:
+                        return_wait(span, way, block, chunk)
+                        total = total + landing[span, spot, r_cuts[chunk]].astype(jnp.float32)
+                    going[span, spot, r_cuts[chunk]] = total.astype(jnp.bfloat16)
+                    return_copy(span, way, block, chunk).start()
+
+    def finish(span, chunk, base, probs, out):
+        spot = place(me)
+        for way in (LEFT, RIGHT):
+            landing = from_left if way == RIGHT else from_right
+            there = me > 0 if way == RIGHT else me < n - 1
+
+            @pl.when(there)
+            def _():
+                return_wait(span, way, me, chunk)
+                part[span, spot, r_cuts[chunk]] += landing[span, spot, r_cuts[chunk]].astype(
+                    jnp.float32
+                )
+
+        out[:, r_cuts[chunk]] = (
+            base(r_cuts[chunk]).astype(jnp.float32) + probs[...] * part[span, spot, r_cuts[chunk]]
+        ).astype(jnp.bfloat16)
+
+    def meta_copy(off):
+        return pltpu.make_async_remote_copy(
+            src_ref=meta.at[lin],
+            dst_ref=meta.at[lin],
+            send_sem=meta_send.at[off],
+            recv_sem=meta_recv.at[off],
+            device_id=peer(off),
+            device_id_type=MESH,
+        )
+
+    def meta_wait(off):
+        other = meta.at[lax.rem(lin + group - off, group)]
+        pltpu.make_async_remote_copy(
+            src_ref=other,
+            dst_ref=other,
+            send_sem=meta_send.at[off],
+            recv_sem=meta_recv.at[off],
+            device_id=peer(group - off),
+            device_id_type=MESH,
+        ).wait_recv()
+
+    shift = pltpu.make_async_remote_copy(
+        src_ref=x_ref,
+        dst_ref=rows_all.at[FWD, place(me), :],
+        send_sem=shift_send,
+        recv_sem=shift_recv,
+        device_id={"section": lax.rem(sec + 1, n_sec)},
+        device_id_type=MESH,
+    )
+
+    gather_start(BWD, 1)
+    shift.start()
+    for off in range(1, group):
+        meta_copy(off).start()
+
+    for hop in range(1, n - 1):
+        for chunk in range(len(g_cuts)):
+            gather_step(BWD, hop, chunk)
+        if hop == 1:
+            for off in range(1, group):
+                meta_wait(off)
+            first = (lax.div(me, sharing) * cap).astype(jnp.float32)
+            owned = jnp.zeros((2, rows), jnp.float32)
+            for other in range(group):
+                slots = meta[other, 0:2, 0:rows] - first
+                owned = owned + jnp.where((slots >= 0.0) & (slots < cap), 1.0, 0.0)
+            owned = jnp.sum(jnp.sum(owned, axis=1, keepdims=True), axis=0, keepdims=True)
+            load_out[...] = owned.astype(jnp.int32)
+
+            def slots_of(span, block):
+                line = meta[block * n_dp + dp, span : span + 1, 0:rows] - first
+                spread = jnp.where(eye, jnp.broadcast_to(line, (rows, rows)), 0.0)
+                return jnp.sum(spread, axis=1, keepdims=True)
+
+            lanes = lax.broadcasted_iota(jnp.int32, (rows, n * cap), 1).astype(jnp.float32)
+            taken = []
+            for block in range(n):
+                slots = slots_of(BWD, block)
+                hit = (slots >= 0.0) & (slots < cap) & (lanes == slots + block * cap)
+                taken.append(jnp.where(hit, 1.0, 0.0))
+            taken = jnp.concatenate(taken, axis=0).astype(jnp.bfloat16)
+            kept = []
+            for block in range(n):
+                slots = slots_of(FWD, block)
+                kept.append(jnp.where((slots >= 0.0) & (slots < cap), 1.0, 0.0))
+            kept = jnp.concatenate(kept, axis=0) > 0.5
+            loads[1].wait()
+            stored = saved[...].astype(jnp.float32)
+            saved_gate = jnp.dot(
+                taken, stored[:, 0, :].astype(jnp.bfloat16), preferred_element_type=jnp.float32
+            )
+            saved_up = jnp.dot(
+                taken, stored[:, 1, :].astype(jnp.bfloat16), preferred_element_type=jnp.float32
+            )
+            sigma = jax.nn.sigmoid(saved_gate)
+            hidden_acc[0] = saved_up * sigma * (1.0 + saved_gate * (1.0 - sigma))
+            hidden_acc[1] = saved_gate * sigma
+
+    shift.wait_recv()
+    gather_start(FWD, 1)
+    loads[0].wait()
+    for chunk, cut in enumerate(g_cuts):
+        gather_step(BWD, n - 1, chunk)
+        term = lax.dot_general(
+            rows_all[BWD, :, cut],
+            down_w[:, cut],
+            contract_last,
+            preferred_element_type=jnp.float32,
+        )
+        if chunk == 0:
+            hidden_acc[2] = term
+        else:
+            hidden_acc[2] += term
+    mid[0] = (hidden_acc[2] * hidden_acc[0]).astype(jnp.bfloat16)
+    mid[1] = (hidden_acc[2] * hidden_acc[1]).astype(jnp.bfloat16)
+
+    loads[2].wait()
+    loads[3].wait()
+
+    def bwd_part(chunk):
+        cut = r_cuts[chunk]
+        part[BWD, :, cut] = lax.dot_general(
+            mid[0], gate_w[cut, :], contract_last, preferred_element_type=jnp.float32
+        ) + lax.dot_general(
+            mid[1], up_w[cut, :], contract_last, preferred_element_type=jnp.float32
+        )
+
+    r_count = len(r_cuts)
+    for chunk in range(r_count):
+        bwd_part(chunk)
+        return_step(BWD, 0, chunk)
+        if chunk == 0:
+            for piece in range(len(g_cuts)):
+                gather_step(FWD, 1, piece)
+    for hop in range(1, n - 1):
+        for chunk in range(r_count):
+            return_step(BWD, hop, chunk)
+        if hop + 1 < n - 1:
+            for piece in range(len(g_cuts)):
+                gather_step(FWD, hop + 1, piece)
+
+    for chunk, cut in enumerate(g_cuts):
+        if n > 2:
+            gather_step(FWD, n - 1, chunk)
+        for at, weights in ((0, gate_w), (1, up_w)):
+            term = jnp.dot(
+                rows_all[FWD, :, cut], weights[cut, :], preferred_element_type=jnp.float32
+            )
+            if chunk == 0:
+                hidden_acc[at] = term
+            else:
+                hidden_acc[at] += term
+    activated = jax.nn.silu(hidden_acc[0]) * hidden_acc[1]
+    mid[0] = jnp.where(kept, activated, 0.0).astype(jnp.bfloat16)
+
+    for chunk in range(r_count):
+        cut = r_cuts[chunk]
+        part[FWD, :, cut] = jnp.dot(mid[0], down_w[:, cut], preferred_element_type=jnp.float32)
+        return_step(FWD, 0, chunk)
+    for chunk in range(r_count):
+        finish(BWD, chunk, lambda cut: cot_ref[:, cut], b_probs, b_out)
+    for hop in range(1, n - 1):
+        for chunk in range(r_count):
+            return_step(FWD, hop, chunk)
+    for chunk in range(r_count):
+        finish(FWD, chunk, lambda cut: rows_all[FWD, place(me), cut], f_probs, f_out)
+
+    shift.wait_send()
+    for off in range(1, group):
+        meta_copy(off).wait_send()
+    for span in (BWD, FWD):
+        for way in (LEFT, RIGHT):
+            for hop in range(1, n):
+
+                @pl.when(gather_sends(way, hop))
+                def _():
+                    for chunk in range(len(g_cuts)):
+                        gather_copy(span, way, hop, chunk).wait_send()
+
+            for block in range(n):
+
+                @pl.when(me > block if way == LEFT else me < block)
+                def _():
+                    for chunk in range(r_count):
+                        return_copy(span, way, block, chunk).wait_send()
+
+
+def relay_fits(fwd_sent, top_count, capacity):
+    rows, width = fwd_sent.shape[1:]
+    return (
+        top_count == 1
+        and capacity == rows
+        and rows % 16 == 0
+        and rows <= 128
+        and width % 256 == 0
+        and lax.axis_size("expert") > 2
+        and lax.axis_size("section") > 1
+    )
+
+
+def relay(
+    fwd_sent,
+    fwd_routes,
+    fwd_probs,
+    backward_cotangent,
+    bwd_routes,
+    bwd_probs,
+    saved_pre,
+    w_gate,
+    w_up,
+    w_down,
+    *,
+    sharing,
+    capacity,
+):
+    n, n_dp, n_sec = (lax.axis_size(name) for name in ("expert", "dp", "section"))
+    rows, width = fwd_sent.shape[1:]
+    hidden = w_gate.shape[2]
+    tokens = n * rows
+    bf16, f32 = jnp.bfloat16, jnp.float32
+    group = n * n_dp
+    g_count = len(cuts(width, GATHER_CHUNKS))
+    r_count = len(cuts(width, RETURN_CHUNKS))
+    vmem = pl.BlockSpec(memory_space=pltpu.VMEM)
+    hbm = pl.BlockSpec(memory_space=pl.ANY)
+    f_next, b_next, load = pl.pallas_call(
+        functools.partial(relay_kernel, (n, n_dp, n_sec, sharing, capacity, rows)),
+        out_shape=(
+            jax.ShapeDtypeStruct((rows, width), bf16),
+            jax.ShapeDtypeStruct((rows, width), bf16),
+            jax.ShapeDtypeStruct((1, 1), jnp.int32),
+        ),
+        in_specs=[vmem] * 6 + [hbm] * 4,
+        out_specs=(vmem, vmem, vmem),
+        scratch_shapes=[
+            pltpu.VMEM((width, hidden), bf16),
+            pltpu.VMEM((width, hidden), bf16),
+            pltpu.VMEM((hidden, width), bf16),
+            pltpu.VMEM(saved_pre.shape[2:], bf16),
+            pltpu.VMEM((2, tokens, width), bf16),
+            pltpu.VMEM((group, 8, 128), f32),
+            pltpu.VMEM((2, tokens, width), bf16),
+            pltpu.VMEM((2, tokens, width), bf16),
+            pltpu.VMEM((2, tokens, width), bf16),
+            pltpu.VMEM((2, tokens, width), f32),
+            pltpu.VMEM((3, tokens, hidden), f32),
+            pltpu.VMEM((2, tokens, hidden), bf16),
+            pltpu.SemaphoreType.DMA((4,)),
+            pltpu.SemaphoreType.DMA,
+            pltpu.SemaphoreType.DMA,
+            pltpu.SemaphoreType.DMA((group,)),
+            pltpu.SemaphoreType.DMA((group,)),
+            pltpu.SemaphoreType.DMA((2, 2, n - 1, g_count)),
+            pltpu.SemaphoreType.DMA((2, 2, n - 1, g_count)),
+            pltpu.SemaphoreType.DMA((2, 2, n, r_count)),
+            pltpu.SemaphoreType.DMA((2, 2, n, r_count)),
+        ],
+        compiler_params=pltpu.CompilerParams(
+            collective_id=0, has_side_effects=True, vmem_limit_bytes=48 * 1024 * 1024
+        ),
+        cost_estimate=pl.CostEstimate(
+            flops=12 * tokens * width * hidden,
+            bytes_accessed=6 * width * hidden,
+            transcendentals=2 * tokens * hidden,
+        ),
+    )(
+        fwd_sent[0],
+        backward_cotangent[0],
+        fwd_routes[0],
+        bwd_routes[0],
+        fwd_probs[0],
+        bwd_probs[0],
+        saved_pre[0, 0],
+        w_gate[0],
+        w_up[0],
+        w_down[0],
+    )
+    return f_next[None], b_next[None], load
 
 
 def shards(
@@ -47,6 +525,21 @@
     top_count = fwd_routes.shape[2]
     capacity = min(token_rows, max(2, 2 * token_rows * top_count // exp_count))
     slot_count = experts * capacity
+    if relay_fits(fwd_sent, top_count, capacity):
+        return relay(
+            fwd_sent,
+            fwd_routes,
+            fwd_probs,
+            backward_cotangent,
+            bwd_routes,
+            bwd_probs,
+            saved_pre,
+            w_gate,
+            w_up,
+            w_down,
+            sharing=sharing,
+            capacity=capacity,
+        )
     arrived = from_behind(fwd_sent, "section", 1)[0]
     gate_mat = w_gate[0]
     up_mat = w_up[0]

time: 76.9 us -> 55.5 us (0.72)
  Pallas kernels: 0 us -> 43.9 us
  waiting for transfers between devices: 19.7 us -> 0 us
  matrix products: 18.1 us -> 0 us
  starting transfers between devices: 16.7 us -> 0 us
  blocking collectives: 13.9 us -> 0 us
  local copies, waits for them, and re-layouts: 3.15 us -> 8.96 us
  other arithmetic: 4.03 us -> 0 us
  between operations: 0.82 us -> 2.39 us
    pallas_call x0 -> x1, Pallas kernels: none -> 43.9 us  [relay(): pl.pallas_call(functools.partial(relay_kernel, (n, n_dp, n_sec, sharing,...]
    all_to_all x4 -> x0, waiting for transfers between devices: 19.7 us -> none  [the longest x2 14.4 us: finish_rows(): lax.all_to_all(result_list.reshape(experts, capacity, width), 'expert', s...]
    dot_general x9 -> x0, matrix products: 18.1 us -> none  [the longest x1 5.43 us: forward_rows(): jnp.dot(hidden_state, down_mat, preferred_element_type=jnp.float32)]
    all_to_all x4 -> x0, starting transfers between devices: 16.7 us -> none  [the longest x2 9.79 us: send_rows(): lax.all_to_all(outgoing, 'expert', split_axis=0, concat_axis=0, tiled=True)]
    psum x1 -> x0, blocking collectives: 13.9 us -> none  [shards(): totals = lax.psum(fwd_count + bwd_count, ('expert', 'dp'))]
    unnamed x11 -> x10, local copies, waits for them, and re-layouts: 0.95 us -> 6.03 us
    squeeze x0 -> x4, local copies, waits for them, and re-layouts: none -> 2.93 us  [the longest x1 0.73 us: relay(): fwd_routes[0]]
    broadcast_in_dim x2 -> x0, local copies, waits for them, and re-layouts: 1.61 us -> none  [send_rows(): jnp.broadcast_to(outgoing, (exp_count, sharing, capacity, width))]
  transfers between devices with their start and end apart: 5 -> 0, of which waited for: 3 -> 0; matrix products, arithmetic and copies ran while one was open for 24% -> 0% of each run, Pallas kernels for 0% -> 0%
where the time goes in v1:
time: 55.5 us; the launch traced here: 55.2 us
  Pallas kernels  43.9 us (79%)
  local copies, waits for them, and re-layouts  8.96 us (16%)
  between operations  2.39 us (4%)
    pallas_call x1, Pallas kernels, relay(): pl.pallas_call(functools.partial(relay_kernel, (n, n_dp, n_sec, sharing,...  43.9 us
    unnamed x10, local copies, waits for them, and re-layouts  6.03 us

profile of v1, /device:TPU:0, one launch (start us, length us, event | category | flops | bytes accessed | tf_op | source)
XLA Modules:
  0.0 55.2 jit_solution(7311156101941811946)
XLA Ops:
  0.6 0.7 %copy.13.f_routes = s32[16,1]{1,0:T(8,128)S(1)} copy(s32[16,1]{0,1:T(1,128)} %bitcast.20) | data formatting | bytes 128 | tf_op jit(solution)/shard_map/squeeze | solution.py:497
  1.4 0.7 %copy.15.f_probs = f32[16,1]{1,0:T(8,128)S(1)} copy(f32[16,1]{0,1:T(1,128)} %bitcast.21) | data formatting | bytes 128 | tf_op jit(solution)/shard_map/squeeze | solution.py:499
  2.1 0.7 %copy.14.b_routes = s32[16,1]{1,0:T(8,128)S(1)} copy(s32[16,1]{0,1:T(1,128)} %bitcast.22) | data formatting | bytes 128 | tf_op jit(solution)/shard_map/squeeze | solution.py:498
  2.8 0.7 %copy.16.b_probs = f32[16,1]{1,0:T(8,128)S(1)} copy(f32[16,1]{0,1:T(1,128)} %bitcast.23) | data formatting | bytes 128 | tf_op jit(solution)/shard_map/squeeze | solution.py:500
  3.6 0.0 copy-start
  3.6 2.0 %copy-done = bf16[1,3584,512]{2,1,0:T(8,128)(2,1)S(1)} copy-done((bf16[1,3584,512]{2,1,0:T(8,128)(2,1)S(1)}, bf16[1,3584,512]{2,1,0:T(8,128)(2,1)}, u32[]{:S(2)}) %copy-start) | copy-done | bytes 3670040
  5.6 0.0 copy-start.1
  5.6 0.9 %copy-done.1 = bf16[1,1,64,2,512]{4,3,2,1,0:T(2,128)(2,1)S(1)} copy-done((bf16[1,1,64,2,512]{4,3,2,1,0:T(2,128)(2,1)S(1)}, bf16[1,1,64,2,512]{4,3,2,1,0:T(2,128)(2,1)}, u32[]{:S(2)}) %copy-start.1) | copy-done | bytes 131096
  6.5 0.0 copy-start.2
  6.5 0.9 %copy-done.2 = bf16[1,16,3584]{2,1,0:T(8,128)(2,1)S(1)} copy-done((bf16[1,16,3584]{2,1,0:T(8,128)(2,1)S(1)}, bf16[1,16,3584]{2,1,0:T(8,128)(2,1)}, u32[]{:S(2)}) %copy-start.2) | copy-done | bytes 114712
  7.4 0.0 copy-start.3
  7.4 0.9 %copy-done.3 = bf16[1,16,3584]{2,1,0:T(8,128)(2,1)S(1)} copy-done((bf16[1,16,3584]{2,1,0:T(8,128)(2,1)S(1)}, bf16[1,16,3584]{2,1,0:T(8,128)(2,1)}, u32[]{:S(2)}) %copy-start.3) | copy-done | bytes 114712
  8.3 43.9 %shard_map.121 = (bf16[16,3584]{1,0:T(8,128)(2,1)S(1)}, bf16[16,3584]{1,0:T(8,128)(2,1)S(1)}, s32[1,1]{1,0:T(1,128)}) custom-call(bf16[16,3584]{1,0:T(8,128)(2,1)S(1)} %bitcast.14, bf16[16,3584]{1,0:T(8,128)(2,1)S(1)} %bitcast.15, s32[16,1]{1,0:T(8,128)S(1)} %copy.13.f_routes, s32[16,1]{1,0:T(8,128)S(1)} %copy.14.b_routes, f32[16,1]{1,0:T(8,128)S(1)} %copy.15.f_probs, ...), custom_call_target="tpu_custom_call" | custom-call | flops 1409286144 | bytes 11010048 | tf_op jit(solution)/shard_map/pallas_call | solution.py:454
  52.2 0.6 %copy.20 = bf16[1,16,3584]{2,1,0:T(8,128)(2,1)} copy(bf16[1,16,3584]{2,1,0:T(8,128)(2,1)S(1)} %bitcast.17) | data formatting | bytes 229376
  52.8 0.6 %copy.21 = bf16[1,16,3584]{2,1,0:T(8,128)(2,1)} copy(bf16[1,16,3584]{2,1,0:T(8,128)(2,1)S(1)} %bitcast.16) | data formatting | bytes 229376
Async XLA Ops:
  3.6 2.0 %copy-start = (bf16[1,3584,512]{2,1,0:T(8,128)(2,1)S(1)}, bf16[1,3584,512]{2,1,0:T(8,128)(2,1)}, u32[]{:S(2)}) copy-start(bf16[1,3584,512]{2,1,0:T(8,128)(2,1)} %param.17) | copy-start | bytes 11010052
  5.6 0.9 %copy-start.1 = (bf16[1,1,64,2,512]{4,3,2,1,0:T(2,128)(2,1)S(1)}, bf16[1,1,64,2,512]{4,3,2,1,0:T(2,128)(2,1)}, u32[]{:S(2)}) copy-start(bf16[1,1,64,2,512]{4,3,2,1,0:T(2,128)(2,1)} %param.16) | copy-start | bytes 393220
  6.5 0.9 %copy-start.2 = (bf16[1,16,3584]{2,1,0:T(8,128)(2,1)S(1)}, bf16[1,16,3584]{2,1,0:T(8,128)(2,1)}, u32[]{:S(2)}) copy-start(bf16[1,16,3584]{2,1,0:T(8,128)(2,1)} %param.10) | copy-start | bytes 344068
  7.4 0.9 %copy-start.3 = (bf16[1,16,3584]{2,1,0:T(8,128)(2,1)S(1)}, bf16[1,16,3584]{2,1,0:T(8,128)(2,1)}, u32[]{:S(2)}) copy-start(bf16[1,16,3584]{2,1,0:T(8,128)(2,1)} %param.13) | copy-start | bytes 344068

commit v2 on v1

--- a/solution.py
+++ b/solution.py
@@ -46,8 +46,8 @@
 
 def relay_kernel(
     size,
-    x_ref,
-    cot_ref,
+    x_hbm,
+    cot_hbm,
     f_routes,
     b_routes,
     f_probs,
@@ -63,6 +63,7 @@
     up_w,
     down_w,
     saved,
+    x_own,
     rows_all,
     meta,
     from_right,
@@ -83,7 +84,7 @@
 ):
     n, n_dp, n_sec, sharing, cap, rows = size
     group = n * n_dp
-    width = cot_ref.shape[1]
+    width = cot_hbm.shape[1]
     me = lax.axis_index("expert")
     dp = lax.axis_index("dp")
     sec = lax.axis_index("section")
@@ -92,17 +93,23 @@
     r_cuts = cuts(width, RETURN_CHUNKS)
     contract_last = (((1,), (1,)), ((), ()))
 
+    def place(block):
+        return pl.ds(pl.multiple_of(block * rows, rows), rows)
+
+    own_rows = [
+        pltpu.make_async_copy(x_hbm, x_own, w_sem.at[4]),
+        pltpu.make_async_copy(cot_hbm, rows_all.at[BWD, place(me), :], w_sem.at[5]),
+    ]
+    for load in own_rows:
+        load.start()
     loads = [
         pltpu.make_async_copy(down_hbm, down_w, w_sem.at[0]),
         pltpu.make_async_copy(saved_hbm, saved, w_sem.at[1]),
         pltpu.make_async_copy(gate_hbm, gate_w, w_sem.at[2]),
         pltpu.make_async_copy(up_hbm, up_w, w_sem.at[3]),
     ]
-    for load in loads:
+    for load in loads[:2]:
         load.start()
-
-    def place(block):
-        return pl.ds(pl.multiple_of(block * rows, rows), rows)
 
     barrier = pltpu.get_barrier_semaphore()
 
@@ -122,15 +129,18 @@
     at_row = lax.broadcasted_iota(jnp.int32, (rows, rows), 0)
     at_col = lax.broadcasted_iota(jnp.int32, (rows, rows), 1)
     eye = at_row == at_col
+
+    def column(line):
+        spread = jnp.where(eye, jnp.broadcast_to(line, (rows, rows)), 0.0)
+        return jnp.sum(spread, axis=1, keepdims=True)
+
     meta[lin] = jnp.zeros(meta.shape[1:], jnp.float32)
     for span, routes in ((FWD, f_routes), (BWD, b_routes)):
-        named = jnp.broadcast_to(routes[...].astype(jnp.float32), (rows, rows))
-        named_row = jnp.sum(jnp.where(eye, named, 0.0), axis=0, keepdims=True)
+        named_row = routes[...].astype(jnp.float32)
+        named = column(named_row)
         earlier = jnp.where((named == named_row) & (at_row < at_col), 1.0, 0.0)
         slot = named_row * cap + jnp.sum(earlier, axis=0, keepdims=True)
         meta[lin, span : span + 1, 0:rows] = slot
-    rows_all[BWD, place(me), :] = cot_ref[...]
-
     pl.semaphore_wait(barrier, group)
 
     def gather_copy(span, way, hop, chunk):
@@ -164,13 +174,12 @@
             device_id_type=MESH,
         ).wait_recv()
 
-    def gather_start(span, hop):
-        for chunk in range(len(g_cuts)):
-            for way in (LEFT, RIGHT):
-
-                @pl.when(gather_sends(way, hop))
-                def _():
-                    gather_copy(span, way, hop, chunk).start()
+    def gather_start(span, hop, chunk):
+        for way in (LEFT, RIGHT):
+
+            @pl.when(gather_sends(way, hop))
+            def _():
+                gather_copy(span, way, hop, chunk).start()
 
     def gather_step(span, hop, chunk):
         for way in (LEFT, RIGHT):
@@ -243,7 +252,7 @@
                 )
 
         out[:, r_cuts[chunk]] = (
-            base(r_cuts[chunk]).astype(jnp.float32) + probs[...] * part[span, spot, r_cuts[chunk]]
+            base(r_cuts[chunk]).astype(jnp.float32) + column(probs[...]) * part[span, spot, r_cuts[chunk]]
         ).astype(jnp.bfloat16)
 
     def meta_copy(off):
@@ -267,17 +276,24 @@
             device_id_type=MESH,
         ).wait_recv()
 
-    shift = pltpu.make_async_remote_copy(
-        src_ref=x_ref,
-        dst_ref=rows_all.at[FWD, place(me), :],
-        send_sem=shift_send,
-        recv_sem=shift_recv,
-        device_id={"section": lax.rem(sec + 1, n_sec)},
-        device_id_type=MESH,
-    )
-
-    gather_start(BWD, 1)
-    shift.start()
+    def shift_copy(chunk):
+        return pltpu.make_async_remote_copy(
+            src_ref=x_own.at[:, g_cuts[chunk]],
+            dst_ref=rows_all.at[FWD, place(me), g_cuts[chunk]],
+            send_sem=shift_send.at[chunk],
+            recv_sem=shift_recv.at[chunk],
+            device_id={"section": lax.rem(sec + 1, n_sec)},
+            device_id_type=MESH,
+        )
+
+    own_rows[0].wait()
+    for chunk in range(len(g_cuts)):
+        shift_copy(chunk).start()
+    own_rows[1].wait()
+    for chunk in range(len(g_cuts)):
+        gather_start(BWD, 1, chunk)
+    for load in loads[2:]:
+        load.start()
     for off in range(1, group):
         meta_copy(off).start()
 
@@ -297,8 +313,7 @@
 
             def slots_of(span, block):
                 line = meta[block * n_dp + dp, span : span + 1, 0:rows] - first
-                spread = jnp.where(eye, jnp.broadcast_to(line, (rows, rows)), 0.0)
-                return jnp.sum(spread, axis=1, keepdims=True)
+                return column(line)
 
             lanes = lax.broadcasted_iota(jnp.int32, (rows, n * cap), 1).astype(jnp.float32)
             taken = []
@@ -324,8 +339,9 @@
             hidden_acc[0] = saved_up * sigma * (1.0 + saved_gate * (1.0 - sigma))
             hidden_acc[1] = saved_gate * sigma
 
-    shift.wait_recv()
-    gather_start(FWD, 1)
+    for chunk in range(len(g_cuts)):
+        shift_copy(chunk).wait_recv()
+        gather_start(FWD, 1, chunk)
     loads[0].wait()
     for chunk, cut in enumerate(g_cuts):
         gather_step(BWD, n - 1, chunk)
@@ -386,14 +402,15 @@
         part[FWD, :, cut] = jnp.dot(mid[0], down_w[:, cut], preferred_element_type=jnp.float32)
         return_step(FWD, 0, chunk)
     for chunk in range(r_count):
-        finish(BWD, chunk, lambda cut: cot_ref[:, cut], b_probs, b_out)
+        finish(BWD, chunk, lambda cut: rows_all[BWD, place(me), cut], b_probs, b_out)
     for hop in range(1, n - 1):
         for chunk in range(r_count):
             return_step(FWD, hop, chunk)
     for chunk in range(r_count):
         finish(FWD, chunk, lambda cut: rows_all[FWD, place(me), cut], f_probs, f_out)
 
-    shift.wait_send()
+    for chunk in range(len(g_cuts)):
+        shift_copy(chunk).wait_send()
     for off in range(1, group):
         meta_copy(off).wait_send()
     for span in (BWD, FWD):
@@ -458,13 +475,14 @@
             jax.ShapeDtypeStruct((rows, width), bf16),
             jax.ShapeDtypeStruct((1, 1), jnp.int32),
         ),
-        in_specs=[vmem] * 6 + [hbm] * 4,
+        in_specs=[hbm] * 2 + [vmem] * 4 + [hbm] * 4,
         out_specs=(vmem, vmem, vmem),
         scratch_shapes=[
             pltpu.VMEM((width, hidden), bf16),
             pltpu.VMEM((width, hidden), bf16),
             pltpu.VMEM((hidden, width), bf16),
             pltpu.VMEM(saved_pre.shape[2:], bf16),
+            pltpu.VMEM((rows, width), bf16),
             pltpu.VMEM((2, tokens, width), bf16),
             pltpu.VMEM((group, 8, 128), f32),
             pltpu.VMEM((2, tokens, width), bf16),
@@ -473,9 +491,9 @@
             pltpu.VMEM((2, tokens, width), f32),
             pltpu.VMEM((3, tokens, hidden), f32),
             pltpu.VMEM((2, tokens, hidden), bf16),
-            pltpu.SemaphoreType.DMA((4,)),
-            pltpu.SemaphoreType.DMA,
-            pltpu.SemaphoreType.DMA,
+            pltpu.SemaphoreType.DMA((6,)),
+            pltpu.SemaphoreType.DMA((g_count,)),
+            pltpu.SemaphoreType.DMA((g_count,)),
             pltpu.SemaphoreType.DMA((group,)),
             pltpu.SemaphoreType.DMA((group,)),
             pltpu.SemaphoreType.DMA((2, 2, n - 1, g_count)),
@@ -484,7 +502,7 @@
             pltpu.SemaphoreType.DMA((2, 2, n, r_count)),
         ],
         compiler_params=pltpu.CompilerParams(
-            collective_id=0, has_side_effects=True, vmem_limit_bytes=48 * 1024 * 1024
+            collective_id=0, has_side_effects=True, vmem_limit_bytes=60 * 1024 * 1024
         ),
         cost_estimate=pl.CostEstimate(
             flops=12 * tokens * width * hidden,
@@ -494,10 +512,10 @@
     )(
         fwd_sent[0],
         backward_cotangent[0],
-        fwd_routes[0],
-        bwd_routes[0],
-        fwd_probs[0],
-        bwd_probs[0],
+        fwd_routes.reshape(1, rows),
+        bwd_routes.reshape(1, rows),
+        fwd_probs.reshape(1, rows),
+        bwd_probs.reshape(1, rows),
         saved_pre[0, 0],
         w_gate[0],
         w_up[0],

time: 55.5 us -> 50.2 us (0.905)
  local copies, waits for them, and re-layouts: 8.96 us -> 3.1 us
  Pallas kernels: 43.9 us -> 44.5 us
    unnamed x10 -> x2, local copies, waits for them, and re-layouts: 6.03 us -> 3.1 us
    squeeze x4 -> x0, local copies, waits for them, and re-layouts: 2.93 us -> none  [the longest x1 0.73 us: relay(): fwd_routes[0]]
    pallas_call x1, Pallas kernels: 43.9 us -> 44.5 us  [relay(): pl.pallas_call(functools.partial(relay_kernel, (n, n_dp, n_sec, sharing,...]
where the time goes in v2:
time: 50.2 us; the launch traced here: 50 us
  Pallas kernels  44.5 us (89%)
  local copies, waits for them, and re-layouts  3.1 us (6%)
  between operations  2.4 us (5%)
    pallas_call x1, Pallas kernels, relay(): pl.pallas_call(functools.partial(relay_kernel, (n, n_dp, n_sec, sharing,...  44.5 us
    unnamed x2, local copies, waits for them, and re-layouts  3.1 us

profile of v2, /device:TPU:0, one launch (start us, length us, event | category | flops | bytes accessed | tf_op | source)
XLA Modules:
  0.0 50.0 jit_solution(4040463159541666447)
XLA Ops:
  0.6 44.5 %shard_map.121 = (bf16[16,3584]{1,0:T(8,128)(2,1)}, bf16[16,3584]{1,0:T(8,128)(2,1)}, s32[1,1]{1,0:T(1,128)}) custom-call(bf16[16,3584]{1,0:T(8,128)(2,1)} %bitcast.16, bf16[16,3584]{1,0:T(8,128)(2,1)} %bitcast.17, s32[1,16]{1,0:T(1,128)} %bitcast.20, s32[1,16]{1,0:T(1,128)} %bitcast.21, f32[1,16]{1,0:T(1,128)} %bitcast.22, f32[1,16]{1,0:T(1,128)} %bitcast.23, ...), custom_call_target="tpu_custom_call" | custom-call | flops 1409286144 | bytes 11010048 | tf_op jit(solution)/shard_map/pallas_call | solution.py:471
  45.2 1.6 %copy.16 = bf16[1,16,3584]{2,1,0:T(8,128)(2,1)} copy(bf16[1,16,3584]{2,1,0:T(8,128)(2,1)} %bitcast.19) | data formatting | bytes 229376
  46.7 1.6 %copy.17 = bf16[1,16,3584]{2,1,0:T(8,128)(2,1)} copy(bf16[1,16,3584]{2,1,0:T(8,128)(2,1)} %bitcast.18) | data formatting | bytes 229376

commit v3 on v2

--- a/solution.py
+++ b/solution.py
@@ -10,8 +10,8 @@
 MESH = pl.DeviceIdType.MESH
 LEFT, RIGHT = 0, 1
 FWD, BWD = 0, 1
-GATHER_CHUNKS = 2
-RETURN_CHUNKS = 2
+GATHER_CHUNKS = 4
+RETURN_CHUNKS = 4
 
 
 def from_behind(array, axis, by):
@@ -38,10 +38,15 @@
     return (placing, weighing, counted)
 
 
-def cuts(width, wanted):
-    count = max(c for c in range(1, wanted + 1) if width % (c * 128) == 0)
-    step = width // count
-    return [pl.ds(i * step, step) for i in range(count)]
+def cuts(width, wanted, small_first):
+    unit = 256
+    count = width // unit
+    pieces = min(wanted, count)
+    sizes = [count // pieces + (1 if i < count % pieces else 0) for i in range(pieces)]
+    if small_first:
+        sizes = sizes[::-1]
+    starts = [sum(sizes[:i]) for i in range(pieces)]
+    return [pl.ds(a * unit, b * unit) for a, b in zip(starts, sizes)]
 
 
 def relay_kernel(
@@ -89,8 +94,8 @@
     dp = lax.axis_index("dp")
     sec = lax.axis_index("section")
     lin = me * n_dp + dp
-    g_cuts = cuts(width, GATHER_CHUNKS)
-    r_cuts = cuts(width, RETURN_CHUNKS)
+    g_cuts = cuts(width, GATHER_CHUNKS, False)
+    r_cuts = cuts(width, RETURN_CHUNKS, True)
     contract_last = (((1,), (1,)), ((), ()))
 
     def place(block):
@@ -252,8 +257,9 @@
                 )
 
         out[:, r_cuts[chunk]] = (
-            base(r_cuts[chunk]).astype(jnp.float32) + column(probs[...]) * part[span, spot, r_cuts[chunk]]
-        ).astype(jnp.bfloat16)
+            base(r_cuts[chunk]).astype(jnp.float32)
+            + column(probs[...]) * part[span, spot, r_cuts[chunk]]
+        )
 
     def meta_copy(off):
         return pltpu.make_async_remote_copy(
@@ -339,9 +345,6 @@
             hidden_acc[0] = saved_up * sigma * (1.0 + saved_gate * (1.0 - sigma))
             hidden_acc[1] = saved_gate * sigma
 
-    for chunk in range(len(g_cuts)):
-        shift_copy(chunk).wait_recv()
-        gather_start(FWD, 1, chunk)
     loads[0].wait()
     for chunk, cut in enumerate(g_cuts):
         gather_step(BWD, n - 1, chunk)
@@ -358,6 +361,9 @@
     mid[0] = (hidden_acc[2] * hidden_acc[0]).astype(jnp.bfloat16)
     mid[1] = (hidden_acc[2] * hidden_acc[1]).astype(jnp.bfloat16)
 
+    for chunk in range(len(g_cuts)):
+        shift_copy(chunk).wait_recv()
+        gather_start(FWD, 1, chunk)
     loads[2].wait()
     loads[3].wait()
 
@@ -369,19 +375,19 @@
             mid[1], up_w[cut, :], contract_last, preferred_element_type=jnp.float32
         )
 
-    r_count = len(r_cuts)
-    for chunk in range(r_count):
-        bwd_part(chunk)
-        return_step(BWD, 0, chunk)
-        if chunk == 0:
-            for piece in range(len(g_cuts)):
-                gather_step(FWD, 1, piece)
+    r_count, g_count = len(r_cuts), len(g_cuts)
+    for chunk in range(max(r_count, g_count)):
+        if chunk < r_count:
+            bwd_part(chunk)
+            return_step(BWD, 0, chunk)
+        if chunk < g_count:
+            gather_step(FWD, 1, chunk)
     for hop in range(1, n - 1):
-        for chunk in range(r_count):
-            return_step(BWD, hop, chunk)
-        if hop + 1 < n - 1:
-            for piece in range(len(g_cuts)):
-                gather_step(FWD, hop + 1, piece)
+        for chunk in range(max(r_count, g_count)):
+            if chunk < g_count and hop + 1 < n - 1:
+                gather_step(FWD, hop + 1, chunk)
+            if chunk < r_count:
+                return_step(BWD, hop, chunk)
 
     for chunk, cut in enumerate(g_cuts):
         if n > 2:
@@ -464,15 +470,15 @@
     tokens = n * rows
     bf16, f32 = jnp.bfloat16, jnp.float32
     group = n * n_dp
-    g_count = len(cuts(width, GATHER_CHUNKS))
-    r_count = len(cuts(width, RETURN_CHUNKS))
+    g_count = len(cuts(width, GATHER_CHUNKS, False))
+    r_count = len(cuts(width, RETURN_CHUNKS, True))
     vmem = pl.BlockSpec(memory_space=pltpu.VMEM)
     hbm = pl.BlockSpec(memory_space=pl.ANY)
     f_next, b_next, load = pl.pallas_call(
         functools.partial(relay_kernel, (n, n_dp, n_sec, sharing, capacity, rows)),
         out_shape=(
-            jax.ShapeDtypeStruct((rows, width), bf16),
-            jax.ShapeDtypeStruct((rows, width), bf16),
+            jax.ShapeDtypeStruct((rows, width), f32),
+            jax.ShapeDtypeStruct((rows, width), f32),
             jax.ShapeDtypeStruct((1, 1), jnp.int32),
         ),
         in_specs=[hbm] * 2 + [vmem] * 4 + [hbm] * 4,
@@ -521,7 +527,7 @@
         w_up[0],
         w_down[0],
     )
-    return f_next[None], b_next[None], load
+    return f_next.astype(bf16)[None], b_next.astype(bf16)[None], load
 
 
 def shards(

time: 50.2 us -> 48.4 us (0.964)
  local copies, waits for them, and re-layouts: 3.1 us -> 0 us
  other arithmetic: 0 us -> 1.76 us
    unnamed x2 -> x0, local copies, waits for them, and re-layouts: 3.1 us -> none
    broadcast_in_dim x0 -> x1, other arithmetic: none -> 1.76 us  [relay(): return (f_next.astype(bf16)[None], b_next.astype(bf16)[None], load)]
where the time goes in v3:
time: 48.4 us; the launch traced here: 48.2 us
  Pallas kernels  44 us (91%)
  between operations  2.4 us (5%)
  other arithmetic  1.76 us (4%)
    pallas_call x1, Pallas kernels, relay(): pl.pallas_call(functools.partial(relay_kernel, (n, n_dp, n_sec, sharing,...  44 us
    broadcast_in_dim x1, other arithmetic, relay(): return (f_next.astype(bf16)[None], b_next.astype(bf16)[None], load)  1.76 us

profile of v3, /device:TPU:0, one launch (start us, length us, event | category | flops | bytes accessed | tf_op | source)
XLA Modules:
  0.0 48.2 jit_solution(7814912649156908720)
XLA Ops:
  0.6 44.0 %shard_map.121 = (f32[16,3584]{1,0:T(8,128)}, f32[16,3584]{1,0:T(8,128)}, s32[1,1]{1,0:T(1,128)}) custom-call(bf16[16,3584]{1,0:T(8,128)(2,1)} %bitcast.18, bf16[16,3584]{1,0:T(8,128)(2,1)} %bitcast.19, s32[1,16]{1,0:T(1,128)} %bitcast.20, s32[1,16]{1,0:T(1,128)} %bitcast.21, f32[1,16]{1,0:T(1,128)} %bitcast.22, f32[1,16]{1,0:T(1,128)} %bitcast.23, ...), custom_call_target="tpu_custom_call" | custom-call | flops 1409286144 | bytes 11010048 | tf_op jit(solution)/shard_map/pallas_call | solution.py:477
  44.7 1.8 %convert_bitcast_fusion = (bf16[1,16,3584]{2,1,0:T(8,128)(2,1)}, bf16[1,16,3584]{2,1,0:T(8,128)(2,1)}) fusion(f32[16,3584]{1,0:T(8,128)} %get-tuple-element.7, f32[16,3584]{1,0:T(8,128)} %get-tuple-element.6), kind=kLoop, calls=%fused_computation | loop fusion | flops 114688 | bytes 688128 | tf_op jit(solution)/shard_map/broadcast_in_dim | solution.py:530

commit v4 on v3

--- a/solution.py
+++ b/solution.py
@@ -76,6 +76,7 @@
     going,
     part,
     hidden_acc,
+    grad_acc,
     mid,
     w_sem,
     shift_send,
@@ -306,7 +307,10 @@
     for hop in range(1, n - 1):
         for chunk in range(len(g_cuts)):
             gather_step(BWD, hop, chunk)
-        if hop == 1:
+        if hop == n - 2:
+            for chunk in range(len(g_cuts)):
+                shift_copy(chunk).wait_recv()
+                gather_start(FWD, 1, chunk)
             for off in range(1, group):
                 meta_wait(off)
             first = (lax.div(me, sharing) * cap).astype(jnp.float32)
@@ -349,31 +353,30 @@
     for chunk, cut in enumerate(g_cuts):
         gather_step(BWD, n - 1, chunk)
         term = lax.dot_general(
+            down_w[:, cut],
             rows_all[BWD, :, cut],
-            down_w[:, cut],
             contract_last,
             preferred_element_type=jnp.float32,
         )
         if chunk == 0:
-            hidden_acc[2] = term
+            grad_acc[...] = term
         else:
-            hidden_acc[2] += term
-    mid[0] = (hidden_acc[2] * hidden_acc[0]).astype(jnp.bfloat16)
-    mid[1] = (hidden_acc[2] * hidden_acc[1]).astype(jnp.bfloat16)
-
-    for chunk in range(len(g_cuts)):
-        shift_copy(chunk).wait_recv()
-        gather_start(FWD, 1, chunk)
+            grad_acc[...] += term
+    grad_hidden = grad_acc[...].T
+    mid[0] = (grad_hidden * hidden_acc[0]).astype(jnp.bfloat16)
+    mid[1] = (grad_hidden * hidden_acc[1]).astype(jnp.bfloat16)
+
     loads[2].wait()
     loads[3].wait()
 
     def bwd_part(chunk):
         cut = r_cuts[chunk]
-        part[BWD, :, cut] = lax.dot_general(
-            mid[0], gate_w[cut, :], contract_last, preferred_element_type=jnp.float32
+        turned = lax.dot_general(
+            gate_w[cut, :], mid[0], contract_last, preferred_element_type=jnp.float32
         ) + lax.dot_general(
-            mid[1], up_w[cut, :], contract_last, preferred_element_type=jnp.float32
-        )
+            up_w[cut, :], mid[1], contract_last, preferred_element_type=jnp.float32
+        )
+        part[BWD, :, cut] = turned.T
 
     r_count, g_count = len(r_cuts), len(g_cuts)
     for chunk in range(max(r_count, g_count)):
@@ -495,7 +498,8 @@
             pltpu.VMEM((2, tokens, width), bf16),
             pltpu.VMEM((2, tokens, width), bf16),
             pltpu.VMEM((2, tokens, width), f32),
-            pltpu.VMEM((3, tokens, hidden), f32),
+            pltpu.VMEM((2, tokens, hidden), f32),
+            pltpu.VMEM((hidden, tokens), f32),
             pltpu.VMEM((2, tokens, hidden), bf16),
             pltpu.SemaphoreType.DMA((6,)),
             pltpu.SemaphoreType.DMA((g_count,)),

time: 48.4 us -> 48 us (level)
  no operation moved by 1% of the time
where the time goes in v4:
time: 48 us; the launch traced here: 47.9 us
  Pallas kernels  43.7 us (91%)
  between operations  2.4 us (5%)
  other arithmetic  1.76 us (4%)
    pallas_call x1, Pallas kernels, relay(): pl.pallas_call(functools.partial(relay_kernel, (n, n_dp, n_sec, sharing,...  43.7 us
    broadcast_in_dim x1, other arithmetic, relay(): return (f_next.astype(bf16)[None], b_next.astype(bf16)[None], load)  1.76 us

profile of v4, /device:TPU:0, one launch (start us, length us, event | category | flops | bytes accessed | tf_op | source)
XLA Modules:
  0.0 47.9 jit_solution(5964669866663957218)
XLA Ops:
  0.6 43.7 %shard_map.121 = (f32[16,3584]{1,0:T(8,128)}, f32[16,3584]{1,0:T(8,128)}, s32[1,1]{1,0:T(1,128)}) custom-call(bf16[16,3584]{1,0:T(8,128)(2,1)} %bitcast.18, bf16[16,3584]{1,0:T(8,128)(2,1)} %bitcast.19, s32[1,16]{1,0:T(1,128)} %bitcast.20, s32[1,16]{1,0:T(1,128)} %bitcast.21, f32[1,16]{1,0:T(1,128)} %bitcast.22, f32[1,16]{1,0:T(1,128)} %bitcast.23, ...), custom_call_target="tpu_custom_call" | custom-call | flops 1409286144 | bytes 11010048 | tf_op jit(solution)/shard_map/pallas_call | solution.py:480
  44.3 1.8 %convert_bitcast_fusion = (bf16[1,16,3584]{2,1,0:T(8,128)(2,1)}, bf16[1,16,3584]{2,1,0:T(8,128)(2,1)}) fusion(f32[16,3584]{1,0:T(8,128)} %get-tuple-element.7, f32[16,3584]{1,0:T(8,128)} %get-tuple-element.6), kind=kLoop, calls=%fused_computation | loop fusion | flops 114688 | bytes 688128 | tf_op jit(solution)/shard_map/broadcast_in_dim | solution.py:534

commit v5 on v4

--- a/solution.py
+++ b/solution.py
@@ -187,11 +187,13 @@
             def _():
                 gather_copy(span, way, hop, chunk).start()
 
+    inner = (me > 0) & (me < n - 1)
+
     def gather_step(span, hop, chunk):
         for way in (LEFT, RIGHT):
             there = me >= hop if way == RIGHT else me + hop < n
 
-            @pl.when(there)
+            @pl.when(there & inner)
             def _():
                 gather_wait(span, way, hop, chunk)
 
@@ -200,6 +202,17 @@
                 @pl.when(gather_sends(way, hop + 1))
                 def _():
                     gather_copy(span, way, hop + 1, chunk).start()
+
+    def gather_rest(span, chunk):
+        @pl.when(me == 0)
+        def _():
+            for hop in range(1, n):
+                gather_wait(span, LEFT, hop, chunk)
+
+        @pl.when(me == n - 1)
+        def _():
+            for hop in range(1, n):
+                gather_wait(span, RIGHT, hop, chunk)
 
     def return_copy(span, way, block, chunk):
         landing = from_left if way == RIGHT else from_right
@@ -351,7 +364,7 @@
 
     loads[0].wait()
     for chunk, cut in enumerate(g_cuts):
-        gather_step(BWD, n - 1, chunk)
+        gather_rest(BWD, chunk)
         term = lax.dot_general(
             down_w[:, cut],
             rows_all[BWD, :, cut],
@@ -385,16 +398,15 @@
             return_step(BWD, 0, chunk)
         if chunk < g_count:
             gather_step(FWD, 1, chunk)
-    for hop in range(1, n - 1):
+    for hop in range(1, n - 2):
         for chunk in range(max(r_count, g_count)):
-            if chunk < g_count and hop + 1 < n - 1:
+            if chunk < g_count:
                 gather_step(FWD, hop + 1, chunk)
             if chunk < r_count:
                 return_step(BWD, hop, chunk)
 
     for chunk, cut in enumerate(g_cuts):
-        if n > 2:
-            gather_step(FWD, n - 1, chunk)
+        gather_rest(FWD, chunk)
         for at, weights in ((0, gate_w), (1, up_w)):
             term = jnp.dot(
                 rows_all[FWD, :, cut], weights[cut, :], preferred_element_type=jnp.float32
@@ -403,6 +415,10 @@
                 hidden_acc[at] = term
             else:
                 hidden_acc[at] += term
+        if chunk < r_count:
+            return_step(BWD, n - 2, chunk)
+    for chunk in range(g_count, r_count):
+        return_step(BWD, n - 2, chunk)
     activated = jax.nn.silu(hidden_acc[0]) * hidden_acc[1]
     mid[0] = jnp.where(kept, activated, 0.0).astype(jnp.bfloat16)
 
@@ -410,11 +426,11 @@
         cut = r_cuts[chunk]
         part[FWD, :, cut] = jnp.dot(mid[0], down_w[:, cut], preferred_element_type=jnp.float32)
         return_step(FWD, 0, chunk)
-    for chunk in range(r_count):
-        finish(BWD, chunk, lambda cut: rows_all[BWD, place(me), cut], b_probs, b_out)
     for hop in range(1, n - 1):
         for chunk in range(r_count):
             return_step(FWD, hop, chunk)
+    for chunk in range(r_count):
+        finish(BWD, chunk, lambda cut: rows_all[BWD, place(me), cut], b_probs, b_out)
     for chunk in range(r_count):
         finish(FWD, chunk, lambda cut: rows_all[FWD, place(me), cut], f_probs, f_out)
 

time: 48 us -> 48.2 us (level)
  no operation moved by 1% of the time
where the time goes in v5:
time: 48.2 us; the launch traced here: 48 us
  Pallas kernels  43.8 us (91%)
  between operations  2.4 us (5%)
  other arithmetic  1.76 us (4%)
    pallas_call x1, Pallas kernels, relay(): pl.pallas_call(functools.partial(relay_kernel, (n, n_dp, n_sec, sharing,...  43.8 us
    broadcast_in_dim x1, other arithmetic, relay(): return (f_next.astype(bf16)[None], b_next.astype(bf16)[None], load)  1.76 us

profile of v5, /device:TPU:0, one launch (start us, length us, event | category | flops | bytes accessed | tf_op | source)
XLA Modules:
  0.0 48.0 jit_solution(11039896749623407413)
XLA Ops:
  0.6 43.8 %shard_map.121 = (f32[16,3584]{1,0:T(8,128)}, f32[16,3584]{1,0:T(8,128)}, s32[1,1]{1,0:T(1,128)}) custom-call(bf16[16,3584]{1,0:T(8,128)(2,1)} %bitcast.18, bf16[16,3584]{1,0:T(8,128)(2,1)} %bitcast.19, s32[1,16]{1,0:T(1,128)} %bitcast.20, s32[1,16]{1,0:T(1,128)} %bitcast.21, f32[1,16]{1,0:T(1,128)} %bitcast.22, f32[1,16]{1,0:T(1,128)} %bitcast.23, ...), custom_call_target="tpu_custom_call" | custom-call | flops 1409286144 | bytes 11010048 | tf_op jit(solution)/shard_map/pallas_call | solution.py:496
  44.4 1.8 %convert_bitcast_fusion = (bf16[1,16,3584]{2,1,0:T(8,128)(2,1)}, bf16[1,16,3584]{2,1,0:T(8,128)(2,1)}) fusion(f32[16,3584]{1,0:T(8,128)} %get-tuple-element.7, f32[16,3584]{1,0:T(8,128)} %get-tuple-element.6), kind=kLoop, calls=%fused_computation | loop fusion | flops 114688 | bytes 688128 | tf_op jit(solution)/shard_map/broadcast_in_dim | solution.py:550

commit v6 on v5

--- a/solution.py
+++ b/solution.py
@@ -240,22 +240,23 @@
             device_id_type=MESH,
         ).wait_recv()
 
-    def return_step(span, hop, chunk):
+    def return_step(span, hop, chunk, nth):
         for way in (LEFT, RIGHT):
             at = n - 1 - hop if way == LEFT else hop
-            blocks = range(at) if way == LEFT else range(n - 1, at, -1)
+            block = nth if way == LEFT else n - 1 - nth
             landing = from_left if way == RIGHT else from_right
 
             @pl.when(me == at)
             def _():
-                for block in blocks:
-                    spot = pl.ds(block * rows, rows)
-                    total = part[span, spot, r_cuts[chunk]]
-                    if hop > 0:
-                        return_wait(span, way, block, chunk)
-                        total = total + landing[span, spot, r_cuts[chunk]].astype(jnp.float32)
-                    going[span, spot, r_cuts[chunk]] = total.astype(jnp.bfloat16)
-                    return_copy(span, way, block, chunk).start()
+                spot = pl.ds(block * rows, rows)
+                total = part[span, spot, r_cuts[chunk]]
+                if hop > 0:
+                    return_wait(span, way, block, chunk)
+                    total = total + landing[span, spot, r_cuts[chunk]].astype(jnp.float32)
+                going[span, spot, r_cuts[chunk]] = total.astype(jnp.bfloat16)
+                return_copy(span, way, block, chunk).start()
+
+    onward = [(nth, hop) for nth in range(n - 1) for hop in range(1, n - 1 - nth)]
 
     def finish(span, chunk, base, probs, out):
         spot = place(me)
@@ -395,15 +396,19 @@
     for chunk in range(max(r_count, g_count)):
         if chunk < r_count:
             bwd_part(chunk)
-            return_step(BWD, 0, chunk)
+            return_step(BWD, 0, chunk, 0)
         if chunk < g_count:
             gather_step(FWD, 1, chunk)
+    for nth in range(1, n - 1):
+        for chunk in range(r_count):
+            return_step(BWD, 0, chunk, nth)
     for hop in range(1, n - 2):
         for chunk in range(max(r_count, g_count)):
             if chunk < g_count:
                 gather_step(FWD, hop + 1, chunk)
             if chunk < r_count:
-                return_step(BWD, hop, chunk)
+                return_step(BWD, hop, chunk, 0)
+    late = [(nth, hop) for nth, hop in onward if nth > 0 or hop == n - 2]
 
     for chunk, cut in enumerate(g_cuts):
         gather_rest(FWD, chunk)
@@ -416,19 +421,24 @@
             else:
                 hidden_acc[at] += term
         if chunk < r_count:
-            return_step(BWD, n - 2, chunk)
+            for nth, hop in late:
+                return_step(BWD, hop, chunk, nth)
     for chunk in range(g_count, r_count):
-        return_step(BWD, n - 2, chunk)
+        for nth, hop in late:
+            return_step(BWD, hop, chunk, nth)
     activated = jax.nn.silu(hidden_acc[0]) * hidden_acc[1]
     mid[0] = jnp.where(kept, activated, 0.0).astype(jnp.bfloat16)
 
     for chunk in range(r_count):
         cut = r_cuts[chunk]
         part[FWD, :, cut] = jnp.dot(mid[0], down_w[:, cut], preferred_element_type=jnp.float32)
-        return_step(FWD, 0, chunk)
-    for hop in range(1, n - 1):
+        return_step(FWD, 0, chunk, 0)
+    for nth in range(1, n - 1):
         for chunk in range(r_count):
-            return_step(FWD, hop, chunk)
+            return_step(FWD, 0, chunk, nth)
+    for nth, hop in onward:
+        for chunk in range(r_count):
+            return_step(FWD, hop, chunk, nth)
     for chunk in range(r_count):
         finish(BWD, chunk, lambda cut: rows_all[BWD, place(me), cut], b_probs, b_out)
     for chunk in range(r_count):

time: 48.2 us -> 47.1 us (0.977)
  Pallas kernels: 43.8 us -> 42.7 us
    pallas_call x1, Pallas kernels: 43.8 us -> 42.7 us  [relay(): pl.pallas_call(functools.partial(relay_kernel, (n, n_dp, n_sec, sharing,...]
where the time goes in v6:
time: 47.1 us; the launch traced here: 46.9 us
  Pallas kernels  42.7 us (91%)
  between operations  2.4 us (5%)
  other arithmetic  1.76 us (4%)
    pallas_call x1, Pallas kernels, relay(): pl.pallas_call(functools.partial(relay_kernel, (n, n_dp, n_sec, sharing,...  42.7 us
    broadcast_in_dim x1, other arithmetic, relay(): return (f_next.astype(bf16)[None], b_next.astype(bf16)[None], load)  1.76 us

profile of v6, /device:TPU:0, one launch (start us, length us, event | category | flops | bytes accessed | tf_op | source)
XLA Modules:
  0.0 46.9 jit_solution(18063898472213857123)
XLA Ops:
  0.6 42.7 %shard_map.121 = (f32[16,3584]{1,0:T(8,128)}, f32[16,3584]{1,0:T(8,128)}, s32[1,1]{1,0:T(1,128)}) custom-call(bf16[16,3584]{1,0:T(8,128)(2,1)} %bitcast.18, bf16[16,3584]{1,0:T(8,128)(2,1)} %bitcast.19, s32[1,16]{1,0:T(1,128)} %bitcast.20, s32[1,16]{1,0:T(1,128)} %bitcast.21, f32[1,16]{1,0:T(1,128)} %bitcast.22, f32[1,16]{1,0:T(1,128)} %bitcast.23, ...), custom_call_target="tpu_custom_call" | custom-call | flops 1409286144 | bytes 11010048 | tf_op jit(solution)/shard_map/pallas_call | solution.py:506
  43.4 1.8 %convert_bitcast_fusion = (bf16[1,16,3584]{2,1,0:T(8,128)(2,1)}, bf16[1,16,3584]{2,1,0:T(8,128)(2,1)}) fusion(f32[16,3584]{1,0:T(8,128)} %get-tuple-element.7, f32[16,3584]{1,0:T(8,128)} %get-tuple-element.6), kind=kLoop, calls=%fused_computation | loop fusion | flops 114688 | bytes 688128 | tf_op jit(solution)/shard_map/broadcast_in_dim | solution.py:560

commit v7 on v6

--- a/solution.py
+++ b/solution.py
@@ -437,10 +437,15 @@
         for chunk in range(r_count):
             return_step(FWD, 0, chunk, nth)
     for nth, hop in onward:
-        for chunk in range(r_count):
-            return_step(FWD, hop, chunk, nth)
+        if nth == 0:
+            for chunk in range(r_count):
+                return_step(FWD, hop, chunk, nth)
     for chunk in range(r_count):
         finish(BWD, chunk, lambda cut: rows_all[BWD, place(me), cut], b_probs, b_out)
+    for nth, hop in onward:
+        if nth > 0:
+            for chunk in range(r_count):
+                return_step(FWD, hop, chunk, nth)
     for chunk in range(r_count):
         finish(FWD, chunk, lambda cut: rows_all[FWD, place(me), cut], f_probs, f_out)
 

time: 47.1 us -> 47.1 us (level)
  no operation moved by 1% of the time
where the time goes in v7:
time: 47.1 us; the launch traced here: 46.9 us
  Pallas kernels  42.7 us (91%)
  between operations  2.4 us (5%)
  other arithmetic  1.76 us (4%)
    pallas_call x1, Pallas kernels, relay(): pl.pallas_call(functools.partial(relay_kernel, (n, n_dp, n_sec, sharing,...  42.7 us
    broadcast_in_dim x1, other arithmetic, relay(): return (f_next.astype(bf16)[None], b_next.astype(bf16)[None], load)  1.76 us

profile of v7, /device:TPU:0, one launch (start us, length us, event | category | flops | bytes accessed | tf_op | source)
XLA Modules:
  0.0 46.9 jit_solution(12185091628227131549)
XLA Ops:
  0.6 42.7 %shard_map.121 = (f32[16,3584]{1,0:T(8,128)}, f32[16,3584]{1,0:T(8,128)}, s32[1,1]{1,0:T(1,128)}) custom-call(bf16[16,3584]{1,0:T(8,128)(2,1)} %bitcast.18, bf16[16,3584]{1,0:T(8,128)(2,1)} %bitcast.19, s32[1,16]{1,0:T(1,128)} %bitcast.20, s32[1,16]{1,0:T(1,128)} %bitcast.21, f32[1,16]{1,0:T(1,128)} %bitcast.22, f32[1,16]{1,0:T(1,128)} %bitcast.23, ...), custom_call_target="tpu_custom_call" | custom-call | flops 1409286144 | bytes 11010048 | tf_op jit(solution)/shard_map/pallas_call | solution.py:511
  43.4 1.8 %convert_bitcast_fusion = (bf16[1,16,3584]{2,1,0:T(8,128)(2,1)}, bf16[1,16,3584]{2,1,0:T(8,128)(2,1)}) fusion(f32[16,3584]{1,0:T(8,128)} %get-tuple-element.7, f32[16,3584]{1,0:T(8,128)} %get-tuple-element.6), kind=kLoop, calls=%fused_computation | loop fusion | flops 114688 | bytes 688128 | tf_op jit(solution)/shard_map/broadcast_in_dim | solution.py:565
